TPU v7x, 512 devices: a whole 4x4x16 slice. The times are simulated.
512 devices in a mesh: grp: 16 (over x, z_hi, core), seq: 32 (over y, z_lo).
Axes of the slice: x: 4, y: 4, z: 16 (z_hi: 2, z_lo: 8; z = z_hi * 8 + z_lo), core: 2. Of those that a mesh axis runs over, the one named last changes fastest.
Arguments:
- x_re: float32 [32, 262144], P(None, ('grp', 'seq')), may hold values from -6 to 6
- x_im: float32 [32, 262144], P(None, ('grp', 'seq')), may hold values from -6 to 6
- gate_in: float32 [32, 262144], P(None, ('grp', 'seq')), may hold values from -6 to 6
- cot_re: float32 [32, 262144], P(None, ('grp', 'seq')), may hold values from -6 to 6
- cot_im: float32 [32, 262144], P(None, ('grp', 'seq')), may hold values from -6 to 6
- filt_re: float32 [32, 512, 512], P('grp', 'seq'), may hold values from -6 to 6
- filt_im: float32 [32, 512, 512], P('grp', 'seq'), may hold values from -6 to 6
Outputs:
- dx_re: float32 [32, 262144], P(None, ('grp', 'seq'))
- dx_im: float32 [32, 262144], P(None, ('grp', 'seq'))
- dgate: float32 [32, 262144], P(None, ('grp', 'seq'))
- dfilt_re: float32 [32, 512, 512], P('grp', 'seq')
- dfilt_im: float32 [32, 512, 512], P('grp', 'seq')
All inputs are finite; a program needn't handle non-finite values.
Results may differ from a plain program's by a relative error of at most 0.000098.
Values sent between devices are 32-bit elements; how exact they have to be, the bound alone decides.
A program may use at most 64 MiB of HBM per device.

v0:
```python
import functools
import math

import jax
import jax.numpy as jnp
import ml_dtypes
import numpy as np
from jax import lax
from jax.experimental import pallas as pl
from jax.experimental.pallas import tpu as pltpu
from jax.sharding import PartitionSpec as P

N1 = 512
N2 = 512
SEQ = N1 * N2
F32 = jnp.float32
BF16 = jnp.bfloat16
MESH = pl.DeviceIdType.MESH
Z_ORDER = (8, 7, 9, 6, 10, 5, 11, 4, 12, 3, 13, 2, 14, 1, 15)


def split_np(table):
    hi = table.astype(ml_dtypes.bfloat16)
    lo = (table - hi.astype(np.float64)).astype(ml_dtypes.bfloat16)
    return np.stack([hi, lo])


def n_of(p, z):
    return (p // 8) * 128 + (z // 8) * 64 + ((p // 4) % 2) * 32 + (p % 4) * 8 + z % 8


def k1_of(p, r):
    return (p % 4) * 128 + (r // 2) * 16 + (p // 4) * 2 + r % 2


def tables():
    idx = np.arange(512)
    n_rows = n_of(idx // 16, idx % 16)
    k_rows = k1_of(idx // 16, idx % 16)
    k_cols = k1_of((idx % 256) // 8, (idx // 256) * 8 + idx % 8)

    def pair(rows, cols, factor):
        angle = (rows[:, None] * cols[None, :] % 512) * (2.0 * math.pi / 512)
        return np.cos(angle) * factor, np.sin(angle) * factor

    unit = 1.0 / math.sqrt(512.0)

    def by_rows(rows, cols, factor):
        c, s = pair(rows, cols, factor)
        return split_np(np.stack([c.reshape(4, 128, 512), s.reshape(4, 128, 512)], 1).reshape(1024, 512))

    first = by_rows(k_rows, n_rows, 2.0 * unit)
    last = by_rows(n_rows, k_cols, 0.5 * unit)
    c, s = pair(idx, idx, unit)
    mid = split_np(np.stack([c.reshape(512, 4, 128), s.reshape(512, 4, 128)], 2).reshape(512, 1024))
    return first, mid, last


def cross(first, second, bit, size):
    low = jnp.where(bit, pltpu.roll(second, size, 1), first)
    high = jnp.where(bit, second, pltpu.roll(first, 128 - size, 1))
    return low, high


def split(value):
    hi = value.astype(BF16)
    return hi, (value - hi.astype(F32)).astype(BF16)


def dot(a, b):
    return jnp.dot(a, b, preferred_element_type=F32)


def kernel(
    x_re, x_im, gate, cot_re, cot_im, filt_re, filt_im, first_hbm, mid_hbm, last_hbm,
    grad, dfilt,
    vx_re, vx_im, vgate, vcot_re, vcot_im, first, mid, last, tw_cos, tw_sin, bend_cos, bend_sin,
    z_out, z_in, p_in, xx, k_out, k_in, dd, fre, fim, df_out, ee, m_out, m_in, xx2, g_out, g_in, v_out, v_in,
    in_sem, tab_sem, send, recv,
):
    grp = lax.axis_index("grp")
    seq = lax.axis_index("seq")
    x, zh, c = grp // 4, (grp // 2) % 2, grp % 2
    y, zl = seq // 8, seq % 8
    z = zh * 8 + zl
    xc = x * 2 + c
    p = xc * 4 + y
    diag = xc == zl

    def dev(p_to, z_to):
        return ((p_to // 8) * 4 + (z_to // 8) * 2 + (p_to // 4) % 2, (p_to % 4) * 8 + z_to % 8)

    bar = pltpu.get_barrier_semaphore()

    def greet(p_to, z_to):
        pl.semaphore_signal(bar, inc=1, device_id=dev(p_to, z_to), device_id_type=MESH)

    loads = [
        pltpu.make_async_copy(src, dst, in_sem.at[i])
        for i, (src, dst) in enumerate(
            ((x_re, vx_re), (x_im, vx_im), (gate, vgate), (cot_re, vcot_re), (cot_im, vcot_im))
        )
    ]
    for load in loads:
        load.start()
    for off in Z_ORDER:
        greet(p, (z + off) % 16)
    for o in range(8):
        @pl.when(jnp.logical_not(diag & (zl == o)))
        def _():
            greet(zl * 4 + y, zh * 8 + o)
            greet(o * 4 + y, zh * 8 + xc)
    for off in range(31, 0, -1):
        greet(p ^ off, z)
    table_loads = [
        pltpu.make_async_copy(src, dst, tab_sem.at[i])
        for i, (src, dst) in enumerate(((first_hbm, first), (mid_hbm, mid), (last_hbm, last)))
    ]
    for load in table_loads:
        load.start()

    lane = lax.broadcasted_iota(jnp.int32, (32, 128), 1)
    row = lax.broadcasted_iota(jnp.int32, (32, 128), 0)
    bit6 = (lane & 64) != 0
    bit5 = (lane & 32) != 0
    bit4 = (lane & 16) != 0
    odd = (row & 1) != 0

    def pair_swap(v):
        up = pltpu.roll(pltpu.roll(v, 31, 0), 16, 1)
        down = pltpu.roll(pltpu.roll(v, 1, 0), 112, 1)
        return jnp.where(odd == bit4, v, jnp.where(odd, down, up))

    for load in loads:
        load.wait()
    for t in range(4):
        cols = pl.ds(t * 128, 128)
        g = vgate[:, cols]
        a = [vx_re[:, cols] * g, vcot_re[:, cols], vx_im[:, cols] * g, vcot_im[:, cols]]
        b = [None] * 4
        b[0], b[2] = cross(a[0], a[2], bit6, 64)
        b[1], b[3] = cross(a[1], a[3], bit6, 64)
        w = [None] * 4
        w[0], w[1] = cross(b[0], b[1], bit5, 32)
        w[2], w[3] = cross(b[2], b[3], bit5, 32)
        for i in range(4):
            z_out[:, i * 4 + t] = pair_swap(w[i]).reshape(4, 8, 128)

    count = 62 - 2 * diag.astype(jnp.int32)
    pl.semaphore_wait(bar, count)

    def z_rows(z_to):
        return (z_to % 8) // 2, (z_to // 8) * 4 + (z_to % 2) * 2

    for off in Z_ORDER:
        z_to = (z + off) % 16
        tile, sub = z_rows(z_to)
        for w in range(2):
            pltpu.make_async_remote_copy(
                z_out.at[tile, :, sub + w], z_in.at[pl.ds(w * 16, 16), z], send.at[0], recv.at[0],
                device_id=dev(p, z_to), device_id_type=MESH,
            ).start()
    tile, sub = z_rows(z)
    for w in range(2):
        pltpu.make_async_copy(z_out.at[tile, :, sub + w], z_in.at[pl.ds(w * 16, 16), z], recv.at[0]).start()

    for o in range(8):
        for src, dst, got in ((filt_re, fre, 6), (filt_im, fim, 8)):
            there = jnp.logical_not(diag & (zl == o))
            @pl.when(there)
            def _():
                pltpu.make_async_remote_copy(
                    src.at[:, pl.ds(2 * o, 2), :], dst.at[:, pl.ds(2 * zl, 2), :], send.at[6], recv.at[got],
                    device_id=dev(o * 4 + y, zh * 8 + xc), device_id_type=MESH,
                ).start()
            @pl.when(jnp.logical_not(there))
            def _():
                pltpu.make_async_copy(
                    src.at[:, pl.ds(2 * o, 2), :], dst.at[:, pl.ds(2 * zl, 2), :], recv.at[got]
                ).start()

    def angles(k, m):
        return (k * m).astype(F32) * (2.0 * math.pi / SEQ)

    sign = jnp.where(lax.broadcasted_iota(jnp.int32, (128, 128), 1) < 64, 1.0, -1.0).astype(F32)
    m_lane = lax.broadcasted_iota(jnp.int32, (128, 128), 1) % 16 + (
        (p % 4) * 128 + ((p // 4) % 4) * 32 + (p // 16) * 16
    )
    for i in range(4):
        k_row = lax.broadcasted_iota(jnp.int32, (128, 128), 0) + i * 128
        theta = angles(k1_of(k_row // 16, k_row % 16), m_lane)
        tw_cos[pl.ds(i * 128, 128), :] = jnp.cos(theta)
        tw_sin[pl.ds(i * 128, 128), :] = jnp.sin(theta) * sign
        theta = angles(k1_of(p, row % 16), lane + i * 128)
        bend_cos[:, pl.ds(i * 128, 128)] = jnp.cos(theta)
        bend_sin[:, pl.ds(i * 128, 128)] = jnp.sin(theta)

    pltpu.make_async_copy(z_in, z_in, recv.at[0]).wait()

    def plane(src, dst, stage, offs):
        for off in offs:
            pltpu.make_async_remote_copy(
                src.at[p ^ off], dst.at[p], send.at[stage], recv.at[stage],
                device_id=dev(p ^ off, z), device_id_type=MESH,
            ).start()

    def plane_self(src, dst, stage):
        pltpu.make_async_copy(src.at[p], dst.at[p], recv.at[stage]).start()

    plane(z_in, p_in, 1, range(31, 0, -1))
    plane_self(z_in, p_in, 1)
    table_loads[0].wait()
    pltpu.make_async_copy(p_in, p_in, recv.at[1]).wait()

    hi, lo = split(p_in[...].reshape(512, 128))
    xx[:, :128] = hi
    xx[:, 128:] = lo
    for i in range(4):
        chunk = (p // 8) ^ i
        rows = pl.ds(pl.multiple_of(chunk * 256, 256), 256)
        out = dot(first[0, rows, :], xx[...]) + dot(first[1, rows, :], xx[...])
        acc = out[:, :128] + out[:, 128:]
        spec = acc[:128] + sign * pltpu.roll(acc[128:], 64, 1)
        half = pl.ds(pl.multiple_of(chunk * 128, 128), 128)
        turned = spec * tw_cos[half, :] + pltpu.roll(spec, 64, 1) * tw_sin[half, :]
        k_out[pl.ds(chunk * 8, 8)] = turned.reshape(8, 16, 128)
        plane(k_out, k_in, 2, range(i * 8 + (i == 0), i * 8 + 8))
        if i == 0:
            plane_self(k_out, k_in, 2)

    table_loads[1].wait()
    pltpu.make_async_copy(k_in, k_in, recv.at[2]).wait()

    mask6, mask5, mask4 = bit6[:16], bit5[:16], bit4[:16]
    for t in range(4):
        v = {}
        for q in range(8):
            v[q] = k_in[(q & 1) * 16 + (q >> 1) * 4 + t]
        a = {}
        for q in range(4):
            a[q], a[q + 4] = cross(v[q], v[q + 4], mask6, 64)
        b = {}
        for q in (0, 1, 4, 5):
            b[q], b[q + 2] = cross(a[q], a[q + 2], mask5, 32)
        for q in (0, 2, 4, 6):
            d = cross(b[q], b[q + 1], mask4, 16)
            for l in range(2):
                hi, lo = split(d[l])
                dd[pl.ds((q + l) * 16, 16), pl.ds(t * 128, 128)] = hi
                dd[pl.ds(128 + (q + l) * 16, 16), pl.ds(t * 128, 128)] = lo

    pltpu.make_async_copy(fre, fre, recv.at[6]).wait()
    pltpu.make_async_copy(fim, fim, recv.at[8]).wait()
    for i in range(4):
        wide = pl.ds(i * 256, 256)
        cols = pl.ds(i * 128, 128)
        out = dot(dd[...], mid[0, :, wide]) + dot(dd[...], mid[1, :, wide])
        acc = out[:128] + out[128:]
        re = acc[:64, :128] + acc[64:, 128:]
        im = acc[64:, :128] - acc[:64, 128:]
        u_re, g_re, u_im, g_im = re[:32], re[32:], im[:32], im[32:]
        df_out[0, :, :, cols] = (g_re * u_re + g_im * u_im).reshape(2, 16, 128)
        df_out[1, :, :, cols] = (g_im * u_re - g_re * u_im).reshape(2, 16, 128)
        f_re = fre[:, :, cols].reshape(32, 128)
        f_im = fim[:, :, cols].reshape(32, 128)
        hi, lo = split(jnp.concatenate([f_re * g_re + f_im * g_im, f_re * g_im - f_im * g_re], 0))
        ee[:64, cols] = hi
        ee[64:, cols] = lo

    mask5_8, mask4_8 = bit5[:8], bit4[:8]
    for t in range(4):
        wide = pl.ds(t * 256, 256)
        cols = pl.ds(t * 128, 128)
        out = dot(ee[...], mid[0, :, wide]) + dot(ee[...], mid[1, :, wide])
        acc = out[:64] + out[64:]
        re = acc[:32, :128] - acc[32:, 128:]
        im = acc[32:, :128] + acc[:32, 128:]
        b_cos, b_sin = bend_cos[:, cols], bend_sin[:, cols]
        bent = cross(re * b_cos - im * b_sin, im * b_cos + re * b_sin, bit6, 64)
        for w2 in range(2):
            v = bent[w2]
            a = [cross(v[l * 16 : l * 16 + 8], v[l * 16 + 8 : l * 16 + 16], mask5_8, 32) for l in range(2)]
            for w1 in range(2):
                d = cross(a[0][w1], a[1][w1], mask4_8, 16)
                for w0 in range(2):
                    m_out[w0 * 16 + w2 * 8 + w1 * 4 + t] = d[w0]

    plane(m_out, m_in, 3, range(31, 0, -1))
    plane_self(m_out, m_in, 3)

    for o in range(8):
        there = jnp.logical_not(diag & (zl == o))
        @pl.when(there)
        def _():
            pltpu.make_async_remote_copy(
                df_out.at[:, :, pl.ds(2 * o, 2), :], dfilt.at[:, :, pl.ds(2 * xc, 2), :], send.at[7], recv.at[7],
                device_id=dev(zl * 4 + y, zh * 8 + o), device_id_type=MESH,
            ).start()
        @pl.when(jnp.logical_not(there))
        def _():
            pltpu.make_async_copy(
                df_out.at[:, :, pl.ds(2 * o, 2), :], dfilt.at[:, :, pl.ds(2 * xc, 2), :], recv.at[7]
            ).start()

    table_loads[2].wait()
    pltpu.make_async_copy(m_in, m_in, recv.at[3]).wait()

    v = m_in[...].reshape(256, 128)
    wide5 = (lax.broadcasted_iota(jnp.int32, (256, 128), 1) & 32) != 0
    hi, lo = split(jnp.where(wide5, pltpu.roll(v, 32, 1), v))
    xx2[:256, :128] = hi
    xx2[:256, 128:] = lo
    hi, lo = split(jnp.where(wide5, v, pltpu.roll(v, 96, 1)))
    xx2[256:, :128] = hi
    xx2[256:, 128:] = lo
    pick5 = (lax.broadcasted_iota(jnp.int32, (8, 8, 128), 2) & 32) != 0
    for i in range(4):
        chunk = (p // 8) ^ i
        rows = pl.ds(pl.multiple_of(chunk * 256, 256), 256)
        out = dot(last[0, rows, :], xx2[...]) + dot(last[1, rows, :], xx2[...])
        acc = out[:, :128] + out[:, 128:]
        g = (acc[:128] - sign * pltpu.roll(acc[128:], 64, 1)).reshape(8, 2, 8, 128)
        g_out[pl.ds(chunk * 8, 8)] = jnp.where(pick5, g[:, 1], g[:, 0])
        plane(g_out, g_in, 4, range(i * 8 + (i == 0), i * 8 + 8))
        if i == 0:
            plane_self(g_out, g_in, 4)
    pltpu.make_async_copy(g_in, g_in, recv.at[4]).wait()

    for w0 in range(2):
        for w2 in range(2):
            at = w0 * 16 + w2 * 8
            a, b = g_in[pl.ds(at, 4)].reshape(32, 128), g_in[pl.ds(at + 4, 4)].reshape(32, 128)
            low, high = cross(a, b, bit5, 32)
            v_out[0, w0, pl.ds(w2 * 4, 4)] = low.reshape(4, 8, 128)
            v_out[1, w0, pl.ds(w2 * 4, 4)] = high.reshape(4, 8, 128)
    for off in Z_ORDER:
        z_to = (z + off) % 16
        for w in range(2):
            pltpu.make_async_remote_copy(
                v_out.at[z_to // 8, w, :, z_to % 8], v_in.at[tile, :, sub + w], send.at[5], recv.at[5],
                device_id=dev(p, z_to), device_id_type=MESH,
            ).start()
    for w in range(2):
        pltpu.make_async_copy(v_out.at[zh, w, :, zl], v_in.at[tile, :, sub + w], recv.at[5]).start()
    pltpu.make_async_copy(v_in, v_in, recv.at[5]).wait()

    for t in range(4):
        a = [pair_swap(v_in[:, w2 * 4 + t].reshape(32, 128)) for w2 in range(2)]
        re, im = cross(a[0], a[1], bit6, 64)
        grad[0, :, pl.ds(t * 128, 128)] = re
        grad[1, :, pl.ds(t * 128, 128)] = im

    pltpu.make_async_copy(dfilt, dfilt, recv.at[7]).wait()

    def sent(ref, stage):
        pltpu.make_async_copy(ref, ref, send.at[stage]).wait()

    sent(z_in.at[pl.ds(0, 30)], 0)
    sent(p_in.at[pl.ds(0, 31)], 1)
    sent(k_in.at[pl.ds(0, 31)], 2)
    sent(m_in.at[pl.ds(0, 31)], 3)
    sent(g_in.at[pl.ds(0, 31)], 4)
    sent(g_in.at[pl.ds(0, 30)], 5)
    for stage in (6, 7):
        @pl.when(diag)
        def _():
            sent(p_in.at[pl.ds(0, 14)], stage)
        @pl.when(jnp.logical_not(diag))
        def _():
            sent(p_in.at[pl.ds(0, 16)], stage)


def per_device(x_re, x_im, gate_in, cot_re, cot_im, filt_re, filt_im):
    first, mid, last = (jnp.asarray(t) for t in tables())
    vm = pltpu.VMEM
    grad, dfilt = pl.pallas_call(
        kernel,
        out_shape=(
            jax.ShapeDtypeStruct((2, 32, 512), F32),
            jax.ShapeDtypeStruct((2, 2, 16, 512), F32),
        ),
        in_specs=[pl.BlockSpec(memory_space=pl.ANY)] * 10,
        out_specs=[pl.BlockSpec(memory_space=pltpu.VMEM)] * 2,
        scratch_shapes=[
            vm((32, 512), F32), vm((32, 512), F32), vm((32, 512), F32), vm((32, 512), F32), vm((32, 512), F32),
            vm((2, 1024, 512), BF16), vm((2, 512, 1024), BF16), vm((2, 1024, 512), BF16),
            vm((512, 128), F32), vm((512, 128), F32), vm((32, 512), F32), vm((32, 512), F32),
            vm((4, 16, 8, 128), F32), vm((32, 16, 128), F32), vm((32, 16, 128), F32), vm((512, 256), BF16),
            vm((32, 16, 128), F32), vm((32, 16, 128), F32), vm((256, 512), BF16),
            vm((2, 16, 512), F32), vm((2, 16, 512), F32), vm((2, 2, 16, 512), F32), vm((128, 512), BF16),
            vm((32, 8, 128), F32), vm((32, 8, 128), F32), vm((512, 256), BF16),
            vm((32, 8, 128), F32), vm((32, 8, 128), F32), vm((2, 2, 8, 8, 128), F32), vm((4, 8, 8, 128), F32),
            pltpu.SemaphoreType.DMA((5,)), pltpu.SemaphoreType.DMA((3,)),
            pltpu.SemaphoreType.DMA((8,)), pltpu.SemaphoreType.DMA((9,)),
        ],
        name="spectral_backward",
        compiler_params=pltpu.CompilerParams(
            collective_id=0, has_side_effects=True, vmem_limit_bytes=60 * 1024 * 1024
        ),
    )(x_re, x_im, gate_in, cot_re, cot_im, filt_re, filt_im, first, mid, last)
    dx_re = gate_in * grad[0]
    dx_im = gate_in * grad[1]
    dgate = x_re * grad[0] + x_im * grad[1]
    return dx_re, dx_im, dgate, dfilt[0] * 0.25, dfilt[1] * 0.25


def solution(mesh):
    seq_in = P(None, ("grp", "seq"))
    filt = P("grp", "seq", None)
    return jax.shard_map(
        per_device,
        mesh=mesh,
        in_specs=(seq_in,) * 5 + (filt,) * 2,
        out_specs=(seq_in,) * 3 + (filt,) * 2,
        check_vma=False,
    )
```

profile of v0, /device:TPU:1, one launch (start us, length us, event | category | flops | bytes accessed | tf_op | source)
XLA Modules:
  0.0 82.3 jit_solution(10060829037324064759)
XLA Ops:
  0.6 0.0 copy-start
  0.6 0.0 copy-start.2
  0.7 0.0 copy-start.1
  0.7 78.5 %spectral_backward.1 = (f32[2,32,512]{2,1,0:T(8,128)}, f32[2,2,16,512]{3,2,1,0:T(8,128)}) custom-call(f32[32,512]{1,0:T(8,128)} %x_re.1, f32[32,512]{1,0:T(8,128)} %x_im.1, f32[32,512]{1,0:T(8,128)} %gate.1, f32[32,512]{1,0:T(8,128)} %cot_re.1, f32[32,512]{1,0:T(8,128)} %cot_im.1, f32[2,16,512]{2,1,0:T(8,128)} %filt_re.1, f32[2,16,512]{2,1,0:T(8,128)} %filt_im.1, ...), custom_call_target="tpu_custom_call" | custom-call | tf_op jit(solution)/shard_map/spectral_backward/pallas_call | solution.py:376
  79.2 0.0 copy-done
  79.2 0.0 copy-done.2
  79.2 0.0 copy-done.1
  79.2 1.6 %bitcast_multiply_fusion.1 = (f32[32,512]{1,0:T(8,128)}, f32[32,512]{1,0:T(8,128)}, f32[32,512]{1,0:T(8,128)}) fusion(f32[32,512]{1,0:T(8,128)S(1)} %copy-done, f32[2,32,512]{2,1,0:T(8,128)} %get-tuple-element.7, f32[32,512]{1,0:T(8,128)S(1)} %copy-done.2, f32[32,512]{1,0:T(8,128)S(1)} %copy-done.1), kind=kLoop, calls=%fused_computation.1 | loop fusion | flops 81920 | bytes 524288 | tf_op jit(solution)/shard_map/mul | solution.py:402
  80.8 1.5 %multiply_bitcast_fusion = (f32[2,16,512]{2,1,0:T(8,128)}, f32[2,16,512]{2,1,0:T(8,128)}) fusion(f32[2,2,16,512]{3,2,1,0:T(8,128)} %get-tuple-element.8), kind=kLoop, calls=%fused_computation.5 | loop fusion | flops 32768 | bytes 262144 | tf_op jit(solution)/shard_map/mul | solution.py:404
Async XLA Ops:
  0.6 78.5 %copy-start = (f32[32,512]{1,0:T(8,128)S(1)}, f32[32,512]{1,0:T(8,128)}, u32[]{:S(2)}) copy-start(f32[32,512]{1,0:T(8,128)} %gate.1) | copy-start | bytes 196612
  0.6 78.5 %copy-start.2 = (f32[32,512]{1,0:T(8,128)S(1)}, f32[32,512]{1,0:T(8,128)}, u32[]{:S(2)}) copy-start(f32[32,512]{1,0:T(8,128)} %x_im.1) | copy-start | bytes 196612
  0.7 78.5 %copy-start.1 = (f32[32,512]{1,0:T(8,128)S(1)}, f32[32,512]{1,0:T(8,128)}, u32[]{:S(2)}) copy-start(f32[32,512]{1,0:T(8,128)} %x_re.1) | copy-start | bytes 196612
where the time goes:
time: 82.5 us; the launch traced here: 82.3 us
  Pallas kernels  78.5 us (95%)
  other arithmetic  3.09 us (4%)
    pallas_call x1, Pallas kernels, per_device(): pl.pallas_call(kernel, out_shape=(jax.ShapeDtypeStruct((2, 32, 512), F32)...  78.5 us

commit v1 on v0

--- a/solution.py
+++ b/solution.py
@@ -73,9 +73,9 @@
 
 def kernel(
     x_re, x_im, gate, cot_re, cot_im, filt_re, filt_im, first_hbm, mid_hbm, last_hbm,
-    grad, dfilt,
+    outs,
     vx_re, vx_im, vgate, vcot_re, vcot_im, first, mid, last, tw_cos, tw_sin, bend_cos, bend_sin,
-    z_out, z_in, p_in, xx, k_out, k_in, dd, fre, fim, df_out, ee, m_out, m_in, xx2, g_out, g_in, v_out, v_in,
+    z_out, z_in, p_in, xx, k_out, k_in, dd, f_mid, f_in, df_out, df_mid, ee, m_out, m_in, xx2, g_out, g_in, v_out, v_in, dfilt,
     in_sem, tab_sem, send, recv,
 ):
     grp = lax.axis_index("grp")
@@ -85,7 +85,6 @@
     z = zh * 8 + zl
     xc = x * 2 + c
     p = xc * 4 + y
-    diag = xc == zl
 
     def dev(p_to, z_to):
         return ((p_to // 8) * 4 + (z_to // 8) * 2 + (p_to // 4) % 2, (p_to % 4) * 8 + z_to % 8)
@@ -105,11 +104,6 @@
         load.start()
     for off in Z_ORDER:
         greet(p, (z + off) % 16)
-    for o in range(8):
-        @pl.when(jnp.logical_not(diag & (zl == o)))
-        def _():
-            greet(zl * 4 + y, zh * 8 + o)
-            greet(o * 4 + y, zh * 8 + xc)
     for off in range(31, 0, -1):
         greet(p ^ off, z)
     table_loads = [
@@ -146,8 +140,7 @@
         for i in range(4):
             z_out[:, i * 4 + t] = pair_swap(w[i]).reshape(4, 8, 128)
 
-    count = 62 - 2 * diag.astype(jnp.int32)
-    pl.semaphore_wait(bar, count)
+    pl.semaphore_wait(bar, 46)
 
     def z_rows(z_to):
         return (z_to % 8) // 2, (z_to // 8) * 4 + (z_to % 2) * 2
@@ -164,20 +157,29 @@
     for w in range(2):
         pltpu.make_async_copy(z_out.at[tile, :, sub + w], z_in.at[pl.ds(w * 16, 16), z], recv.at[0]).start()
 
-    for o in range(8):
-        for src, dst, got in ((filt_re, fre, 6), (filt_im, fim, 8)):
-            there = jnp.logical_not(diag & (zl == o))
-            @pl.when(there)
-            def _():
+    def spread_plane(pairs, stage):
+        for off in (7, 5, 3, 6, 4, 2, 1):
+            for src, dst in pairs:
                 pltpu.make_async_remote_copy(
-                    src.at[:, pl.ds(2 * o, 2), :], dst.at[:, pl.ds(2 * zl, 2), :], send.at[6], recv.at[got],
-                    device_id=dev(o * 4 + y, zh * 8 + xc), device_id_type=MESH,
+                    src.at[..., pl.ds(2 * (xc ^ off), 2), :], dst.at[..., pl.ds(2 * xc, 2), :],
+                    send.at[stage], recv.at[stage], device_id=dev(p ^ (off * 4), z), device_id_type=MESH,
                 ).start()
-            @pl.when(jnp.logical_not(there))
-            def _():
-                pltpu.make_async_copy(
-                    src.at[:, pl.ds(2 * o, 2), :], dst.at[:, pl.ds(2 * zl, 2), :], recv.at[got]
-                ).start()
+        for src, dst in pairs:
+            pltpu.make_async_copy(
+                src.at[..., pl.ds(2 * xc, 2), :], dst.at[..., pl.ds(2 * xc, 2), :], recv.at[stage]
+            ).start()
+
+    def spread_line(src, dst, stage):
+        for off in range(7, 0, -1):
+            pltpu.make_async_remote_copy(
+                src.at[..., pl.ds(2 * (zl ^ off), 2), :], dst.at[..., pl.ds(2 * zl, 2), :],
+                send.at[stage], recv.at[stage], device_id=dev(p, z ^ off), device_id_type=MESH,
+            ).start()
+        pltpu.make_async_copy(
+            src.at[..., pl.ds(2 * zl, 2), :], dst.at[..., pl.ds(2 * zl, 2), :], recv.at[stage]
+        ).start()
+
+    spread_plane(((filt_re, f_mid.at[0]), (filt_im, f_mid.at[1])), 6)
 
     def angles(k, m):
         return (k * m).astype(F32) * (2.0 * math.pi / SEQ)
@@ -209,6 +211,8 @@
 
     plane(z_in, p_in, 1, range(31, 0, -1))
     plane_self(z_in, p_in, 1)
+    pltpu.make_async_copy(f_mid, f_mid, recv.at[6]).wait()
+    spread_line(f_mid, f_in, 7)
     table_loads[0].wait()
     pltpu.make_async_copy(p_in, p_in, recv.at[1]).wait()
 
@@ -249,8 +253,7 @@
                 dd[pl.ds((q + l) * 16, 16), pl.ds(t * 128, 128)] = hi
                 dd[pl.ds(128 + (q + l) * 16, 16), pl.ds(t * 128, 128)] = lo
 
-    pltpu.make_async_copy(fre, fre, recv.at[6]).wait()
-    pltpu.make_async_copy(fim, fim, recv.at[8]).wait()
+    pltpu.make_async_copy(f_in, f_in, recv.at[7]).wait()
     for i in range(4):
         wide = pl.ds(i * 256, 256)
         cols = pl.ds(i * 128, 128)
@@ -261,11 +264,12 @@
         u_re, g_re, u_im, g_im = re[:32], re[32:], im[:32], im[32:]
         df_out[0, :, :, cols] = (g_re * u_re + g_im * u_im).reshape(2, 16, 128)
         df_out[1, :, :, cols] = (g_im * u_re - g_re * u_im).reshape(2, 16, 128)
-        f_re = fre[:, :, cols].reshape(32, 128)
-        f_im = fim[:, :, cols].reshape(32, 128)
+        f_re = f_in[0, :, :, cols].reshape(32, 128)
+        f_im = f_in[1, :, :, cols].reshape(32, 128)
         hi, lo = split(jnp.concatenate([f_re * g_re + f_im * g_im, f_re * g_im - f_im * g_re], 0))
         ee[:64, cols] = hi
         ee[64:, cols] = lo
+    spread_line(df_out, df_mid, 8)
 
     mask5_8, mask4_8 = bit5[:8], bit4[:8]
     for t in range(4):
@@ -287,20 +291,6 @@
 
     plane(m_out, m_in, 3, range(31, 0, -1))
     plane_self(m_out, m_in, 3)
-
-    for o in range(8):
-        there = jnp.logical_not(diag & (zl == o))
-        @pl.when(there)
-        def _():
-            pltpu.make_async_remote_copy(
-                df_out.at[:, :, pl.ds(2 * o, 2), :], dfilt.at[:, :, pl.ds(2 * xc, 2), :], send.at[7], recv.at[7],
-                device_id=dev(zl * 4 + y, zh * 8 + o), device_id_type=MESH,
-            ).start()
-        @pl.when(jnp.logical_not(there))
-        def _():
-            pltpu.make_async_copy(
-                df_out.at[:, :, pl.ds(2 * o, 2), :], dfilt.at[:, :, pl.ds(2 * xc, 2), :], recv.at[7]
-            ).start()
 
     table_loads[2].wait()
     pltpu.make_async_copy(m_in, m_in, recv.at[3]).wait()
@@ -342,15 +332,18 @@
             ).start()
     for w in range(2):
         pltpu.make_async_copy(v_out.at[zh, w, :, zl], v_in.at[tile, :, sub + w], recv.at[5]).start()
+    pltpu.make_async_copy(df_mid, df_mid, recv.at[8]).wait()
+    spread_plane(((df_mid, dfilt),), 9)
     pltpu.make_async_copy(v_in, v_in, recv.at[5]).wait()
 
     for t in range(4):
         a = [pair_swap(v_in[:, w2 * 4 + t].reshape(32, 128)) for w2 in range(2)]
         re, im = cross(a[0], a[1], bit6, 64)
-        grad[0, :, pl.ds(t * 128, 128)] = re
-        grad[1, :, pl.ds(t * 128, 128)] = im
-
-    pltpu.make_async_copy(dfilt, dfilt, recv.at[7]).wait()
+        outs[0, :, pl.ds(t * 128, 128)] = re
+        outs[1, :, pl.ds(t * 128, 128)] = im
+
+    pltpu.make_async_copy(dfilt, dfilt, recv.at[9]).wait()
+    outs[2:] = dfilt[...].reshape(2, 32, 512)
 
     def sent(ref, stage):
         pltpu.make_async_copy(ref, ref, send.at[stage]).wait()
@@ -361,47 +354,41 @@
     sent(m_in.at[pl.ds(0, 31)], 3)
     sent(g_in.at[pl.ds(0, 31)], 4)
     sent(g_in.at[pl.ds(0, 30)], 5)
-    for stage in (6, 7):
-        @pl.when(diag)
-        def _():
-            sent(p_in.at[pl.ds(0, 14)], stage)
-        @pl.when(jnp.logical_not(diag))
-        def _():
-            sent(p_in.at[pl.ds(0, 16)], stage)
+    for stage in (6, 7, 8, 9):
+        sent(p_in.at[pl.ds(0, 14)], stage)
 
 
 def per_device(x_re, x_im, gate_in, cot_re, cot_im, filt_re, filt_im):
     first, mid, last = (jnp.asarray(t) for t in tables())
     vm = pltpu.VMEM
-    grad, dfilt = pl.pallas_call(
+    outs = pl.pallas_call(
         kernel,
-        out_shape=(
-            jax.ShapeDtypeStruct((2, 32, 512), F32),
-            jax.ShapeDtypeStruct((2, 2, 16, 512), F32),
-        ),
+        out_shape=jax.ShapeDtypeStruct((4, 32, 512), F32),
         in_specs=[pl.BlockSpec(memory_space=pl.ANY)] * 10,
-        out_specs=[pl.BlockSpec(memory_space=pltpu.VMEM)] * 2,
+        out_specs=pl.BlockSpec(memory_space=pltpu.VMEM),
         scratch_shapes=[
             vm((32, 512), F32), vm((32, 512), F32), vm((32, 512), F32), vm((32, 512), F32), vm((32, 512), F32),
             vm((2, 1024, 512), BF16), vm((2, 512, 1024), BF16), vm((2, 1024, 512), BF16),
             vm((512, 128), F32), vm((512, 128), F32), vm((32, 512), F32), vm((32, 512), F32),
             vm((4, 16, 8, 128), F32), vm((32, 16, 128), F32), vm((32, 16, 128), F32), vm((512, 256), BF16),
             vm((32, 16, 128), F32), vm((32, 16, 128), F32), vm((256, 512), BF16),
-            vm((2, 16, 512), F32), vm((2, 16, 512), F32), vm((2, 2, 16, 512), F32), vm((128, 512), BF16),
+            vm((2, 2, 16, 512), F32), vm((2, 2, 16, 512), F32), vm((2, 2, 16, 512), F32), vm((2, 2, 16, 512), F32), vm((128, 512), BF16),
             vm((32, 8, 128), F32), vm((32, 8, 128), F32), vm((512, 256), BF16),
-            vm((32, 8, 128), F32), vm((32, 8, 128), F32), vm((2, 2, 8, 8, 128), F32), vm((4, 8, 8, 128), F32),
+            vm((32, 8, 128), F32), vm((32, 8, 128), F32), vm((2, 2, 8, 8, 128), F32), vm((4, 8, 8, 128), F32), vm((2, 2, 16, 512), F32),
             pltpu.SemaphoreType.DMA((5,)), pltpu.SemaphoreType.DMA((3,)),
-            pltpu.SemaphoreType.DMA((8,)), pltpu.SemaphoreType.DMA((9,)),
+            pltpu.SemaphoreType.DMA((10,)), pltpu.SemaphoreType.DMA((10,)),
         ],
         name="spectral_backward",
         compiler_params=pltpu.CompilerParams(
             collective_id=0, has_side_effects=True, vmem_limit_bytes=60 * 1024 * 1024
         ),
     )(x_re, x_im, gate_in, cot_re, cot_im, filt_re, filt_im, first, mid, last)
-    dx_re = gate_in * grad[0]
-    dx_im = gate_in * grad[1]
-    dgate = x_re * grad[0] + x_im * grad[1]
-    return dx_re, dx_im, dgate, dfilt[0] * 0.25, dfilt[1] * 0.25
+    dx_re = gate_in * outs[0]
+    dx_im = gate_in * outs[1]
+    dgate = x_re * outs[0] + x_im * outs[1]
+    dfilt_re = (outs[2] * 0.25).reshape(filt_re.shape)
+    dfilt_im = (outs[3] * 0.25).reshape(filt_im.shape)
+    return dx_re, dx_im, dgate, dfilt_re, dfilt_im
 
 
 def solution(mesh):

time: 82.5 us -> 71.3 us (0.86)
  Pallas kernels: 78.5 us -> 67.2 us
    pallas_call x1, Pallas kernels: 78.5 us -> 67.2 us  [per_device(): pl.pallas_call(kernel, out_shape=jax.ShapeDtypeStruct((4, 32, 512), F32),...]
where the time goes in v1:
time: 71.3 us; the launch traced here: 71 us
  Pallas kernels  67.2 us (94%)
  other arithmetic  3.09 us (4%)
    pallas_call x1, Pallas kernels, per_device(): pl.pallas_call(kernel, out_shape=jax.ShapeDtypeStruct((4, 32, 512), F32),...  67.2 us
    mul x1, other arithmetic, per_device(): dx_im = gate_in * outs[1]  1.56 us
    mul x1, other arithmetic, per_device(): dfilt_im = (outs[3] * 0.25).reshape(filt_im.shape)  1.53 us

profile of v1, /device:TPU:1, one launch (start us, length us, event | category | flops | bytes accessed | tf_op | source)
XLA Modules:
  0.0 71.0 jit_solution(12424569606146171086)
XLA Ops:
  0.6 0.0 copy-start.1
  0.6 0.0 copy-start.2
  0.7 0.0 copy-start
  0.7 67.2 %spectral_backward.1 = f32[4,32,512]{2,1,0:T(8,128)} custom-call(f32[32,512]{1,0:T(8,128)} %x_re.1, f32[32,512]{1,0:T(8,128)} %x_im.1, f32[32,512]{1,0:T(8,128)} %gate.1, f32[32,512]{1,0:T(8,128)} %cot_re.1, f32[32,512]{1,0:T(8,128)} %cot_im.1, f32[2,16,512]{2,1,0:T(8,128)} %filt_re.1, f32[2,16,512]{2,1,0:T(8,128)} %filt_im.1, ...), custom_call_target="tpu_custom_call" | custom-call | tf_op jit(solution)/shard_map/spectral_backward/pallas_call | solution.py:364
  67.9 0.0 copy-done.1
  67.9 0.0 copy-done.2
  67.9 0.0 copy-done
  67.9 1.6 %bitcast_multiply_fusion.1 = (f32[32,512]{1,0:T(8,128)}, f32[32,512]{1,0:T(8,128)}, f32[32,512]{1,0:T(8,128)}) fusion(f32[32,512]{1,0:T(8,128)S(1)} %copy-done, f32[4,32,512]{2,1,0:T(8,128)} %spectral_backward.1, f32[32,512]{1,0:T(8,128)S(1)} %copy-done.2, f32[32,512]{1,0:T(8,128)S(1)} %copy-done.1), kind=kLoop, calls=%fused_computation.1 | loop fusion | flops 81920 | bytes 524288 | tf_op jit(solution)/shard_map/mul | solution.py:387
  69.5 1.5 %slice_multiply_fusion = (f32[1,32,512]{2,1,0:T(8,128)}, f32[1,32,512]{2,1,0:T(8,128)}) fusion(f32[4,32,512]{2,1,0:T(8,128)} %spectral_backward.1), kind=kLoop, calls=%fused_computation.5 | loop fusion | flops 32768 | bytes 262144 | tf_op jit(solution)/shard_map/mul | solution.py:390
Async XLA Ops:
  0.6 67.3 %copy-start.1 = (f32[32,512]{1,0:T(8,128)S(1)}, f32[32,512]{1,0:T(8,128)}, u32[]{:S(2)}) copy-start(f32[32,512]{1,0:T(8,128)} %x_re.1) | copy-start | bytes 196612
  0.6 67.3 %copy-start.2 = (f32[32,512]{1,0:T(8,128)S(1)}, f32[32,512]{1,0:T(8,128)}, u32[]{:S(2)}) copy-start(f32[32,512]{1,0:T(8,128)} %x_im.1) | copy-start | bytes 196612
  0.7 67.3 %copy-start = (f32[32,512]{1,0:T(8,128)S(1)}, f32[32,512]{1,0:T(8,128)}, u32[]{:S(2)}) copy-start(f32[32,512]{1,0:T(8,128)} %gate.1) | copy-start | bytes 196612

commit v2 on v1

v2 whole, which is shorter than its diff:
```python
import functools
import math

import jax
import jax.numpy as jnp
import ml_dtypes
import numpy as np
from jax import lax
from jax.experimental import pallas as pl
from jax.experimental.pallas import tpu as pltpu
from jax.sharding import PartitionSpec as P

N1 = 512
N2 = 512
SEQ = N1 * N2
F32 = jnp.float32
BF16 = jnp.bfloat16
MESH = pl.DeviceIdType.MESH
Z_ORDER = (8, 7, 9, 6, 10, 5, 11, 4, 12, 3, 13, 2, 14, 1, 15)


def split_np(table):
    hi = table.astype(ml_dtypes.bfloat16)
    lo = (table - hi.astype(np.float64)).astype(ml_dtypes.bfloat16)
    return np.stack([hi, lo])


def n_of(p, z):
    return ((p % 16) // 4) * 128 + (z // 8) * 64 + (p // 16) * 32 + (p % 4) * 8 + z % 8


def k1_of(q, r):
    return (q % 4) * 128 + (r // 4) * 16 + (q // 4) * 4 + r % 4


def tables():
    idx = np.arange(512)
    n_rows = n_of(idx // 16, idx % 16)
    n_cols = n_of((idx % 256) // 8, (idx % 8) * 2 + idx // 256)
    k_rows = k1_of(idx // 32, idx % 32)
    k_cols = k1_of((idx % 256) // 16, (idx // 256) * 16 + idx % 16)

    def pair(rows, cols, factor):
        angle = (rows[:, None] * cols[None, :] % 512) * (2.0 * math.pi / 512)
        return np.cos(angle) * factor, np.sin(angle) * factor

    unit = 1.0 / math.sqrt(512.0)

    def by_rows(rows, cols, factor):
        c, s = pair(rows, cols, factor)
        return split_np(np.stack([c.reshape(4, 128, 512), s.reshape(4, 128, 512)], 1).reshape(1024, 512))

    first = by_rows(k_rows, n_cols, 2.0 * unit)
    last = by_rows(n_rows, k_cols, 0.5 * unit)
    c, s = pair(idx, idx, unit)
    mid = split_np(np.stack([c.reshape(512, 4, 128), s.reshape(512, 4, 128)], 2).reshape(512, 1024))
    return first, mid, last


def cross(first, second, bit, size):
    low = jnp.where(bit, pltpu.roll(second, size, 1), first)
    high = jnp.where(bit, second, pltpu.roll(first, 128 - size, 1))
    return low, high


def split(value):
    hi = value.astype(BF16)
    return hi, (value - hi.astype(F32)).astype(BF16)


def dot(a, b):
    return jnp.dot(a, b, preferred_element_type=F32)


def kernel(
    x_re, x_im, gate, cot_re, cot_im, filt_re, filt_im, first_hbm, mid_hbm, last_hbm,
    outs,
    vx_re, vx_im, vgate, vcot_re, vcot_im, first, mid, last, tw_cos, tw_sin, bend_cos, bend_sin,
    z_out, z_in, p_in, part, xx, k_out, k_in, dd, f_mid, f_in, df_out, df_mid, ee, m_out, m_in, xx2, g_out, g_in, v_out, v_in, dfilt,
    in_sem, tab_sem, send, recv,
):
    grp = lax.axis_index("grp")
    seq = lax.axis_index("seq")
    x, zh, c = grp // 4, (grp // 2) % 2, grp % 2
    y, zl = seq // 8, seq % 8
    z = zh * 8 + zl
    xc = x * 2 + c
    q = x * 4 + y
    p = c * 16 + q
    near = z % 2
    far = 1 - near

    def dev(p_to, z_to):
        return (((p_to // 4) % 4) * 4 + (z_to // 8) * 2 + p_to // 16, (p_to % 4) * 8 + z_to % 8)

    bar = pltpu.get_barrier_semaphore()

    def greet(p_to, z_to):
        pl.semaphore_signal(bar, inc=1, device_id=dev(p_to, z_to), device_id_type=MESH)

    loads = [
        pltpu.make_async_copy(src, dst, in_sem.at[i])
        for i, (src, dst) in enumerate(
            ((x_re, vx_re), (x_im, vx_im), (gate, vgate), (cot_re, vcot_re), (cot_im, vcot_im))
        )
    ]
    for load in loads:
        load.start()
    for off in Z_ORDER:
        greet(p, (z + off) % 16)
    for off in range(31, 0, -1):
        greet(p ^ off, z)
    table_loads = [
        pltpu.make_async_copy(src, dst, tab_sem.at[i])
        for i, (src, dst) in enumerate(((first_hbm, first), (mid_hbm, mid), (last_hbm, last)))
    ]
    for load in table_loads:
        load.start()

    lane = lax.broadcasted_iota(jnp.int32, (32, 128), 1)
    row = lax.broadcasted_iota(jnp.int32, (32, 128), 0)
    bit6 = (lane & 64) != 0
    bit5 = (lane & 32) != 0

    for load in loads:
        load.wait()
    for t in range(4):
        cols = pl.ds(t * 128, 128)
        g = vgate[:, cols]
        a = [vx_re[:, cols] * g, vcot_re[:, cols], vx_im[:, cols] * g, vcot_im[:, cols]]
        b = [None] * 4
        b[0], b[2] = cross(a[0], a[2], bit6, 64)
        b[1], b[3] = cross(a[1], a[3], bit6, 64)
        w = [None] * 4
        w[0], w[1] = cross(b[0], b[1], bit5, 32)
        w[2], w[3] = cross(b[2], b[3], bit5, 32)
        for i in range(4):
            z_out[:, i * 4 + t] = w[i].reshape(4, 8, 128)

    pl.semaphore_wait(bar, 46)

    def z_rows(z_to):
        return (z_to % 8) // 2, (z_to // 8) * 4 + (z_to % 2) * 2

    for off in Z_ORDER:
        stage = 0 if off % 2 else 10
        z_to = (z + off) % 16
        tile, sub = z_rows(z_to)
        for l in range(2):
            pltpu.make_async_remote_copy(
                z_out.at[tile, :, sub + l], z_in.at[near, pl.ds(l * 16, 16), z // 2],
                send.at[stage], recv.at[stage], device_id=dev(p, z_to), device_id_type=MESH,
            ).start()
    tile, sub = z_rows(z)
    for l in range(2):
        pltpu.make_async_copy(z_out.at[tile, :, sub + l], z_in.at[near, pl.ds(l * 16, 16), z // 2], recv.at[10]).start()

    def own_rows(k):
        return pl.ds(4 * k, 4)

    def plane_step(stage, moves):
        for off in (7, 5, 3, 6, 4, 2, 1, 0):
            other = xc ^ off
            for src, dst in moves(other // 2, other % 2, other):
                if off:
                    pltpu.make_async_remote_copy(
                        src, dst, send.at[stage], recv.at[stage],
                        device_id=dev((other % 2) * 16 + (other // 2) * 4 + y, z), device_id_type=MESH,
                    ).start()
                else:
                    pltpu.make_async_copy(src, dst, recv.at[stage]).start()

    def line_step(src, dst, stage):
        for off in range(7, 0, -1):
            pltpu.make_async_remote_copy(
                src.at[:, own_rows(zl ^ off), :], dst.at[:, own_rows(zl), :],
                send.at[stage], recv.at[stage], device_id=dev(p, z ^ off), device_id_type=MESH,
            ).start()
        pltpu.make_async_copy(src.at[:, own_rows(zl), :], dst.at[:, own_rows(zl), :], recv.at[stage]).start()

    plane_step(
        6,
        lambda x_to, c_to, xc_to: (
            (filt_re.at[c_to, own_rows(x_to), :], f_mid.at[0, own_rows(xc), :]),
            (filt_im.at[c_to, own_rows(x_to), :], f_mid.at[1, own_rows(xc), :]),
        ),
    )

    def angles(k, m):
        return (k * m).astype(F32) * (2.0 * math.pi / SEQ)

    sign = jnp.where(lax.broadcasted_iota(jnp.int32, (128, 128), 1) < 64, 1.0, -1.0).astype(F32)
    m_lane = lax.broadcasted_iota(jnp.int32, (128, 128), 1) % 32 + (y * 128 + x * 32)
    for i in range(4):
        k_row = lax.broadcasted_iota(jnp.int32, (128, 128), 0) + i * 128
        theta = angles(k1_of(k_row // 32, k_row % 32), m_lane)
        tw_cos[pl.ds(i * 128, 128), :] = jnp.cos(theta)
        tw_sin[pl.ds(i * 128, 128), :] = jnp.sin(theta) * sign
        theta = angles(k1_of(q, row), lane + i * 128)
        bend_cos[:, pl.ds(i * 128, 128)] = jnp.cos(theta)
        bend_sin[:, pl.ds(i * 128, 128)] = jnp.sin(theta)

    def plane(src, dst, stage, offs, own):
        for off in offs:
            pltpu.make_async_remote_copy(
                src.at[p ^ off], dst.at[p], send.at[stage], recv.at[stage],
                device_id=dev(p ^ off, z), device_id_type=MESH,
            ).start()
        if own:
            pltpu.make_async_copy(src.at[p], dst.at[p], recv.at[stage]).start()

    def chips(src, dst, stage, offs, own):
        for off in offs:
            pltpu.make_async_remote_copy(
                src.at[q ^ off], dst.at[q], send.at[stage], recv.at[stage],
                device_id=dev(p ^ off, z), device_id_type=MESH,
            ).start()
        if own:
            pltpu.make_async_copy(src.at[q], dst.at[q], recv.at[stage]).start()

    halves = ((far, 0, 1), (near, 10, 11))
    for half, got, stage in halves:
        pltpu.make_async_copy(z_in.at[half], z_in.at[half], recv.at[got]).wait()
        plane(z_in.at[half], p_in.at[half], stage, range(31, 0, -1), True)
    pltpu.make_async_copy(f_mid, f_mid, recv.at[6]).wait()
    line_step(f_mid, f_in, 7)

    table_loads[0].wait()
    for at, (half, got, stage) in enumerate(halves):
        pltpu.make_async_copy(p_in.at[half], p_in.at[half], recv.at[stage]).wait()
        hi, lo = split(p_in[half].reshape(256, 128))
        xx[at, :, :128] = hi
        xx[at, :, 128:] = lo
        depth = pl.ds(pl.multiple_of(half * 256, 256), 256)
        for i in range(4):
            chunk = (q // 4) ^ i
            rows = pl.ds(pl.multiple_of(chunk * 256, 256), 256)
            out = dot(first[0, rows, depth], xx[at]) + dot(first[1, rows, depth], xx[at])
            acc = out[:, :128] + out[:, 128:]
            if at == 0:
                part[i] = acc
                continue
            acc = acc + part[i]
            spec = acc[:128] + sign * pltpu.roll(acc[128:], 64, 1)
            rows = pl.ds(pl.multiple_of(chunk * 128, 128), 128)
            turned = spec * tw_cos[rows, :] + pltpu.roll(spec, 64, 1) * tw_sin[rows, :]
            k_out[pl.ds(chunk * 4, 4)] = turned.reshape(4, 32, 128)
            chips(k_out, k_in, 2, range(i * 4 + (i == 0), i * 4 + 4), i == 0)

    table_loads[1].wait()
    pltpu.make_async_copy(k_in, k_in, recv.at[2]).wait()

    for t in range(4):
        cols = pl.ds(t * 128, 128)
        a = [cross(k_in[w1 * 4 + t], k_in[8 + w1 * 4 + t], bit6, 64) for w1 in range(2)]
        for ri in range(2):
            b = cross(a[0][ri], a[1][ri], bit5, 32)
            for ug in range(2):
                hi, lo = split(b[ug])
                dd[pl.ds(ri * 64 + ug * 32, 32), cols] = hi
                dd[pl.ds(128 + ri * 64 + ug * 32, 32), cols] = lo

    pltpu.make_async_copy(f_in, f_in, recv.at[7]).wait()
    for i in range(4):
        wide = pl.ds(i * 256, 256)
        cols = pl.ds(i * 128, 128)
        out = dot(dd[...], mid[0, :, wide]) + dot(dd[...], mid[1, :, wide])
        acc = out[:128] + out[128:]
        re = acc[:64, :128] + acc[64:, 128:]
        im = acc[64:, :128] - acc[:64, 128:]
        u_re, g_re, u_im, g_im = re[:32], re[32:], im[:32], im[32:]
        df_out[0, :, cols] = g_re * u_re + g_im * u_im
        df_out[1, :, cols] = g_im * u_re - g_re * u_im
        f_re = f_in[0, :, cols]
        f_im = f_in[1, :, cols]
        hi, lo = split(jnp.concatenate([f_re * g_re + f_im * g_im, f_re * g_im - f_im * g_re], 0))
        ee[:64, cols] = hi
        ee[64:, cols] = lo
    line_step(df_out, df_mid, 8)

    mask5 = bit5[:16]
    for t in range(4):
        wide = pl.ds(t * 256, 256)
        cols = pl.ds(t * 128, 128)
        out = dot(ee[...], mid[0, :, wide]) + dot(ee[...], mid[1, :, wide])
        acc = out[:64] + out[64:]
        re = acc[:32, :128] - acc[32:, 128:]
        im = acc[32:, :128] + acc[:32, 128:]
        b_cos, b_sin = bend_cos[:, cols], bend_sin[:, cols]
        bent = cross(re * b_cos - im * b_sin, im * b_cos + re * b_sin, bit6, 64)
        for w2 in range(2):
            d = cross(bent[w2][:16], bent[w2][16:], mask5, 32)
            for w1 in range(2):
                m_out[w2 * 8 + w1 * 4 + t] = d[w1]

    chips(m_out, m_in, 3, range(15, 0, -1), True)

    table_loads[2].wait()
    pltpu.make_async_copy(m_in, m_in, recv.at[3]).wait()

    v = m_in[...].reshape(256, 128)
    wide5 = (lax.broadcasted_iota(jnp.int32, (256, 128), 1) & 32) != 0
    hi, lo = split(jnp.where(wide5, pltpu.roll(v, 32, 1), v))
    xx2[:256, :128] = hi
    xx2[:256, 128:] = lo
    hi, lo = split(jnp.where(wide5, v, pltpu.roll(v, 96, 1)))
    xx2[256:, :128] = hi
    xx2[256:, 128:] = lo
    pick5 = (lax.broadcasted_iota(jnp.int32, (8, 8, 128), 2) & 32) != 0
    for i in range(4):
        chunk = (p // 8) ^ i
        rows = pl.ds(pl.multiple_of(chunk * 256, 256), 256)
        out = dot(last[0, rows, :], xx2[...]) + dot(last[1, rows, :], xx2[...])
        acc = out[:, :128] + out[:, 128:]
        g = (acc[:128] - sign * pltpu.roll(acc[128:], 64, 1)).reshape(8, 2, 8, 128)
        g_out[pl.ds(chunk * 8, 8)] = jnp.where(pick5, g[:, 1], g[:, 0])
        plane(g_out, g_in, 4, range(i * 8 + (i == 0), i * 8 + 8), i == 0)
    pltpu.make_async_copy(g_in, g_in, recv.at[4]).wait()

    for l in range(2):
        for w2 in range(2):
            at = l * 16 + w2 * 8
            a, b = g_in[pl.ds(at, 4)].reshape(32, 128), g_in[pl.ds(at + 4, 4)].reshape(32, 128)
            low, high = cross(a, b, bit5, 32)
            v_out[0, l, pl.ds(w2 * 4, 4)] = low.reshape(4, 8, 128)
            v_out[1, l, pl.ds(w2 * 4, 4)] = high.reshape(4, 8, 128)
    for off in Z_ORDER:
        z_to = (z + off) % 16
        for l in range(2):
            pltpu.make_async_remote_copy(
                v_out.at[z_to // 8, l, :, z_to % 8], v_in.at[tile, :, sub + l], send.at[5], recv.at[5],
                device_id=dev(p, z_to), device_id_type=MESH,
            ).start()
    for l in range(2):
        pltpu.make_async_copy(v_out.at[zh, l, :, zl], v_in.at[tile, :, sub + l], recv.at[5]).start()
    pltpu.make_async_copy(df_mid, df_mid, recv.at[8]).wait()
    plane_step(
        9, lambda x_to, c_to, xc_to: ((df_mid.at[:, own_rows(xc_to), :], dfilt.at[:, c, own_rows(x), :]),)
    )
    pltpu.make_async_copy(v_in, v_in, recv.at[5]).wait()

    for t in range(4):
        a = [v_in[:, w2 * 4 + t].reshape(32, 128) for w2 in range(2)]
        re, im = cross(a[0], a[1], bit6, 64)
        outs[0, :, pl.ds(t * 128, 128)] = re
        outs[1, :, pl.ds(t * 128, 128)] = im

    pltpu.make_async_copy(dfilt, dfilt, recv.at[9]).wait()
    outs[2:] = dfilt[...].reshape(2, 32, 512)

    def sent(ref, stage):
        pltpu.make_async_copy(ref, ref, send.at[stage]).wait()

    sent(z_in.at[0], 0)
    sent(z_in.at[0, pl.ds(0, 28)], 10)
    for stage in (1, 11):
        sent(z_in.at[0, pl.ds(0, 31)], stage)
    sent(k_in.at[pl.ds(0, 15)], 2)
    sent(m_in.at[pl.ds(0, 15)], 3)
    sent(g_in.at[pl.ds(0, 31)], 4)
    sent(g_in.at[pl.ds(0, 30)], 5)
    for stage in (6, 7, 8, 9):
        sent(m_in.at[pl.ds(0, 14)], stage)


def finish(x_re, x_im, gate, outs, dx_re, dx_im, dgate, dfilt_re, dfilt_im):
    dx_re[...] = gate[...] * outs[0]
    dx_im[...] = gate[...] * outs[1]
    dgate[...] = x_re[...] * outs[0] + x_im[...] * outs[1]
    dfilt_re[...] = (outs[2] * 0.25).reshape(2, 16, 512)
    dfilt_im[...] = (outs[3] * 0.25).reshape(2, 16, 512)


def per_device(x_re, x_im, gate_in, cot_re, cot_im, filt_re, filt_im):
    first, mid, last = (jnp.asarray(t) for t in tables())
    vm = pltpu.VMEM
    outs = pl.pallas_call(
        kernel,
        out_shape=jax.ShapeDtypeStruct((4, 32, 512), F32),
        in_specs=[pl.BlockSpec(memory_space=pl.ANY)] * 10,
        out_specs=pl.BlockSpec(memory_space=pltpu.VMEM),
        scratch_shapes=[
            vm((32, 512), F32), vm((32, 512), F32), vm((32, 512), F32), vm((32, 512), F32), vm((32, 512), F32),
            vm((2, 1024, 512), BF16), vm((2, 512, 1024), BF16), vm((2, 1024, 512), BF16),
            vm((512, 128), F32), vm((512, 128), F32), vm((32, 512), F32), vm((32, 512), F32),
            vm((4, 16, 8, 128), F32), vm((2, 32, 8, 128), F32), vm((2, 32, 8, 128), F32), vm((4, 256, 128), F32),
            vm((2, 256, 256), BF16), vm((16, 32, 128), F32), vm((16, 32, 128), F32), vm((256, 512), BF16),
            vm((2, 32, 512), F32), vm((2, 32, 512), F32), vm((2, 32, 512), F32), vm((2, 32, 512), F32),
            vm((128, 512), BF16), vm((16, 16, 128), F32), vm((16, 16, 128), F32), vm((512, 256), BF16),
            vm((32, 8, 128), F32), vm((32, 8, 128), F32), vm((2, 2, 8, 8, 128), F32), vm((4, 8, 8, 128), F32),
            vm((2, 2, 16, 512), F32),
            pltpu.SemaphoreType.DMA((5,)), pltpu.SemaphoreType.DMA((3,)),
            pltpu.SemaphoreType.DMA((12,)), pltpu.SemaphoreType.DMA((12,)),
        ],
        name="spectral_backward",
        compiler_params=pltpu.CompilerParams(
            collective_id=0, has_side_effects=True, vmem_limit_bytes=60 * 1024 * 1024
        ),
    )(x_re, x_im, gate_in, cot_re, cot_im, filt_re, filt_im, first, mid, last)
    vmem = pl.BlockSpec(memory_space=pltpu.VMEM)
    wide = jax.ShapeDtypeStruct((32, 512), F32)
    return pl.pallas_call(
        finish,
        out_shape=(wide, wide, wide) + (jax.ShapeDtypeStruct(filt_re.shape, F32),) * 2,
        in_specs=[vmem] * 4,
        out_specs=(vmem,) * 5,
        name="products",
    )(x_re, x_im, gate_in, outs)


def solution(mesh):
    seq_in = P(None, ("grp", "seq"))
    filt = P("grp", "seq", None)
    return jax.shard_map(
        per_device,
        mesh=mesh,
        in_specs=(seq_in,) * 5 + (filt,) * 2,
        out_specs=(seq_in,) * 3 + (filt,) * 2,
        check_vma=False,
    )
```

time: 71.3 us -> 69.4 us (0.973)
  other arithmetic: 3.09 us -> 0 us
  Pallas kernels: 67.2 us -> 68.6 us
    mul x2 -> x0, other arithmetic: 3.09 us -> none  [the longest x1 1.56 us: per_device(): dx_im = gate_in * outs[1]]
    pallas_call x0 -> x1, Pallas kernels: none -> 1.79 us  [per_device(): pl.pallas_call(finish, out_shape=(wide, wide, wide) + (jax.ShapeDtypeStru...]
where the time goes in v2:
time: 69.4 us; the launch traced here: 69.2 us
  Pallas kernels  68.6 us (99%)
    pallas_call x1, Pallas kernels, per_device(): pl.pallas_call(kernel, out_shape=jax.ShapeDtypeStruct((4, 32, 512), F32),...  66.8 us
    pallas_call x1, Pallas kernels, per_device(): pl.pallas_call(finish, out_shape=(wide, wide, wide) + (jax.ShapeDtypeStru...  1.79 us

profile of v2, /device:TPU:1, one launch (start us, length us, event | category | flops | bytes accessed | tf_op | source)
XLA Modules:
  0.0 69.2 jit_solution(12906982897435831126)
XLA Ops:
  0.6 66.8 %spectral_backward.1.outs = f32[4,32,512]{2,1,0:T(8,128)} custom-call(f32[32,512]{1,0:T(8,128)} %x_re.3, f32[32,512]{1,0:T(8,128)} %x_im.3, f32[32,512]{1,0:T(8,128)} %gate.3, f32[32,512]{1,0:T(8,128)} %cot_re.1, f32[32,512]{1,0:T(8,128)} %cot_im.1, f32[2,16,512]{2,1,0:T(8,128)} %filt_re.1, f32[2,16,512]{2,1,0:T(8,128)} %filt_im.1, ...), custom_call_target="tpu_custom_call" | custom-call | tf_op jit(solution)/shard_map/spectral_backward/pallas_call | solution.py:377
  67.4 1.8 %products.1 = (f32[32,512]{1,0:T(8,128)}, f32[32,512]{1,0:T(8,128)}, f32[32,512]{1,0:T(8,128)}, f32[2,16,512]{2,1,0:T(8,128)}, f32[2,16,512]{2,1,0:T(8,128)}) custom-call(f32[32,512]{1,0:T(8,128)} %x_re.3, f32[32,512]{1,0:T(8,128)} %x_im.3, f32[32,512]{1,0:T(8,128)} %gate.3, f32[4,32,512]{2,1,0:T(8,128)} %spectral_backward.1.outs), custom_call_target="tpu_custom_call" | custom-call | tf_op jit(solution)/shard_map/products/pallas_call | solution.py:402

commit v3 on v2

--- a/solution.py
+++ b/solution.py
@@ -76,7 +76,7 @@
     x_re, x_im, gate, cot_re, cot_im, filt_re, filt_im, first_hbm, mid_hbm, last_hbm,
     outs,
     vx_re, vx_im, vgate, vcot_re, vcot_im, first, mid, last, tw_cos, tw_sin, bend_cos, bend_sin,
-    z_out, z_in, p_in, part, xx, k_out, k_in, dd, f_mid, f_in, df_out, df_mid, ee, m_out, m_in, xx2, g_out, g_in, v_out, v_in, dfilt,
+    z_out, z_in, p_in, part, xx, k_out, k_in, dd, g_keep, f_mid, f_in, df_out, df_mid, ee, m_out, m_in, xx2, g_out, g_in, v_out, v_in, dfilt,
     in_sem, tab_sem, send, recv,
 ):
     grp = lax.axis_index("grp")
@@ -257,26 +257,26 @@
             b = cross(a[0][ri], a[1][ri], bit5, 32)
             for ug in range(2):
                 hi, lo = split(b[ug])
-                dd[pl.ds(ri * 64 + ug * 32, 32), cols] = hi
-                dd[pl.ds(128 + ri * 64 + ug * 32, 32), cols] = lo
+                dd[ug, pl.ds(ri * 32, 32), cols] = hi
+                dd[ug, pl.ds(64 + ri * 32, 32), cols] = lo
+
+    def spectrum(which, i):
+        wide = pl.ds(i * 256, 256)
+        out = dot(dd[which], mid[0, :, wide]) + dot(dd[which], mid[1, :, wide])
+        acc = out[:64] + out[64:]
+        return acc[:32, :128] + acc[32:, 128:], acc[32:, :128] - acc[:32, 128:]
 
     pltpu.make_async_copy(f_in, f_in, recv.at[7]).wait()
     for i in range(4):
-        wide = pl.ds(i * 256, 256)
         cols = pl.ds(i * 128, 128)
-        out = dot(dd[...], mid[0, :, wide]) + dot(dd[...], mid[1, :, wide])
-        acc = out[:128] + out[128:]
-        re = acc[:64, :128] + acc[64:, 128:]
-        im = acc[64:, :128] - acc[:64, 128:]
-        u_re, g_re, u_im, g_im = re[:32], re[32:], im[:32], im[32:]
-        df_out[0, :, cols] = g_re * u_re + g_im * u_im
-        df_out[1, :, cols] = g_im * u_re - g_re * u_im
+        g_re, g_im = spectrum(1, i)
+        g_keep[0, :, cols] = g_re
+        g_keep[1, :, cols] = g_im
         f_re = f_in[0, :, cols]
         f_im = f_in[1, :, cols]
         hi, lo = split(jnp.concatenate([f_re * g_re + f_im * g_im, f_re * g_im - f_im * g_re], 0))
         ee[:64, cols] = hi
         ee[64:, cols] = lo
-    line_step(df_out, df_mid, 8)
 
     mask5 = bit5[:16]
     for t in range(4):
@@ -294,6 +294,14 @@
                 m_out[w2 * 8 + w1 * 4 + t] = d[w1]
 
     chips(m_out, m_in, 3, range(15, 0, -1), True)
+
+    for i in range(4):
+        cols = pl.ds(i * 128, 128)
+        u_re, u_im = spectrum(0, i)
+        g_re, g_im = g_keep[0, :, cols], g_keep[1, :, cols]
+        df_out[0, :, cols] = g_re * u_re + g_im * u_im
+        df_out[1, :, cols] = g_im * u_re - g_re * u_im
+    line_step(df_out, df_mid, 8)
 
     table_loads[2].wait()
     pltpu.make_async_copy(m_in, m_in, recv.at[3]).wait()
@@ -384,7 +392,8 @@
             vm((2, 1024, 512), BF16), vm((2, 512, 1024), BF16), vm((2, 1024, 512), BF16),
             vm((512, 128), F32), vm((512, 128), F32), vm((32, 512), F32), vm((32, 512), F32),
             vm((4, 16, 8, 128), F32), vm((2, 32, 8, 128), F32), vm((2, 32, 8, 128), F32), vm((4, 256, 128), F32),
-            vm((2, 256, 256), BF16), vm((16, 32, 128), F32), vm((16, 32, 128), F32), vm((256, 512), BF16),
+            vm((2, 256, 256), BF16), vm((16, 32, 128), F32), vm((16, 32, 128), F32), vm((2, 128, 512), BF16),
+            vm((2, 32, 512), F32),
             vm((2, 32, 512), F32), vm((2, 32, 512), F32), vm((2, 32, 512), F32), vm((2, 32, 512), F32),
             vm((128, 512), BF16), vm((16, 16, 128), F32), vm((16, 16, 128), F32), vm((512, 256), BF16),
             vm((32, 8, 128), F32), vm((32, 8, 128), F32), vm((2, 2, 8, 8, 128), F32), vm((4, 8, 8, 128), F32),

time: 69.4 us -> 69 us (level)
  no operation moved by 1% of the time
where the time goes in v3:
time: 69 us; the launch traced here: 68.9 us
  Pallas kernels  68.2 us (99%)
    pallas_call x1, Pallas kernels, per_device(): pl.pallas_call(kernel, out_shape=jax.ShapeDtypeStruct((4, 32, 512), F32),...  66.4 us
    pallas_call x1, Pallas kernels, per_device(): pl.pallas_call(finish, out_shape=(wide, wide, wide) + (jax.ShapeDtypeStru...  1.79 us

profile of v3, /device:TPU:1, one launch (start us, length us, event | category | flops | bytes accessed | tf_op | source)
XLA Modules:
  0.0 68.9 jit_solution(4081568321107602339)
XLA Ops:
  0.6 66.4 %spectral_backward.1.outs = f32[4,32,512]{2,1,0:T(8,128)} custom-call(f32[32,512]{1,0:T(8,128)} %x_re.3, f32[32,512]{1,0:T(8,128)} %x_im.3, f32[32,512]{1,0:T(8,128)} %gate.3, f32[32,512]{1,0:T(8,128)} %cot_re.1, f32[32,512]{1,0:T(8,128)} %cot_im.1, f32[2,16,512]{2,1,0:T(8,128)} %filt_re.1, f32[2,16,512]{2,1,0:T(8,128)} %filt_im.1, ...), custom_call_target="tpu_custom_call" | custom-call | tf_op jit(solution)/shard_map/spectral_backward/pallas_call | solution.py:385
  67.1 1.8 %products.1 = (f32[32,512]{1,0:T(8,128)}, f32[32,512]{1,0:T(8,128)}, f32[32,512]{1,0:T(8,128)}, f32[2,16,512]{2,1,0:T(8,128)}, f32[2,16,512]{2,1,0:T(8,128)}) custom-call(f32[32,512]{1,0:T(8,128)} %x_re.3, f32[32,512]{1,0:T(8,128)} %x_im.3, f32[32,512]{1,0:T(8,128)} %gate.3, f32[4,32,512]{2,1,0:T(8,128)} %spectral_backward.1.outs), custom_call_target="tpu_custom_call" | custom-call | tf_op jit(solution)/shard_map/products/pallas_call | solution.py:411

commit v4 on v3

--- a/solution.py
+++ b/solution.py
@@ -135,7 +135,8 @@
         w[0], w[1] = cross(b[0], b[1], bit5, 32)
         w[2], w[3] = cross(b[2], b[3], bit5, 32)
         for i in range(4):
-            z_out[:, i * 4 + t] = w[i].reshape(4, 8, 128)
+            for tile in range(4):
+                z_out[pl.ds(tile * 128 + i * 4 + t, 8, stride=16), :] = w[i][tile * 8 : tile * 8 + 8]
 
     pl.semaphore_wait(bar, 46)
 
@@ -146,14 +147,12 @@
         stage = 0 if off % 2 else 10
         z_to = (z + off) % 16
         tile, sub = z_rows(z_to)
-        for l in range(2):
-            pltpu.make_async_remote_copy(
-                z_out.at[tile, :, sub + l], z_in.at[near, pl.ds(l * 16, 16), z // 2],
-                send.at[stage], recv.at[stage], device_id=dev(p, z_to), device_id_type=MESH,
-            ).start()
+        pltpu.make_async_remote_copy(
+            z_out.at[pl.ds(tile * 128 + sub * 16, 32), :], z_in.at[near, z // 2],
+            send.at[stage], recv.at[stage], device_id=dev(p, z_to), device_id_type=MESH,
+        ).start()
     tile, sub = z_rows(z)
-    for l in range(2):
-        pltpu.make_async_copy(z_out.at[tile, :, sub + l], z_in.at[near, pl.ds(l * 16, 16), z // 2], recv.at[10]).start()
+    pltpu.make_async_copy(z_out.at[pl.ds(tile * 128 + sub * 16, 32), :], z_in.at[near, z // 2], recv.at[10]).start()
 
     def own_rows(k):
         return pl.ds(4 * k, 4)
@@ -221,7 +220,12 @@
     halves = ((far, 0, 1), (near, 10, 11))
     for half, got, stage in halves:
         pltpu.make_async_copy(z_in.at[half], z_in.at[half], recv.at[got]).wait()
-        plane(z_in.at[half], p_in.at[half], stage, range(31, 0, -1), True)
+        for off in (26, 22, 25, 27, 30, 10, 18, 21, 23, 24, 29, 31, 6, 9, 11, 14, 17, 19, 20, 28, 2, 5, 7, 8, 13, 15, 16, 1, 3, 4, 12):
+            pltpu.make_async_remote_copy(
+                z_in.at[half, :, p ^ off], p_in.at[half, p], send.at[stage], recv.at[stage],
+                device_id=dev(p ^ off, z), device_id_type=MESH,
+            ).start()
+        pltpu.make_async_copy(z_in.at[half, :, p], p_in.at[half, p], recv.at[stage]).start()
     pltpu.make_async_copy(f_mid, f_mid, recv.at[6]).wait()
     line_step(f_mid, f_in, 7)
 
@@ -360,9 +364,9 @@
         pltpu.make_async_copy(ref, ref, send.at[stage]).wait()
 
     sent(z_in.at[0], 0)
-    sent(z_in.at[0, pl.ds(0, 28)], 10)
+    sent(z_in.at[0, pl.ds(0, 7)], 10)
     for stage in (1, 11):
-        sent(z_in.at[0, pl.ds(0, 31)], stage)
+        sent(p_in.at[0, pl.ds(0, 31)], stage)
     sent(k_in.at[pl.ds(0, 15)], 2)
     sent(m_in.at[pl.ds(0, 15)], 3)
     sent(g_in.at[pl.ds(0, 31)], 4)
@@ -391,7 +395,7 @@
             vm((32, 512), F32), vm((32, 512), F32), vm((32, 512), F32), vm((32, 512), F32), vm((32, 512), F32),
             vm((2, 1024, 512), BF16), vm((2, 512, 1024), BF16), vm((2, 1024, 512), BF16),
             vm((512, 128), F32), vm((512, 128), F32), vm((32, 512), F32), vm((32, 512), F32),
-            vm((4, 16, 8, 128), F32), vm((2, 32, 8, 128), F32), vm((2, 32, 8, 128), F32), vm((4, 256, 128), F32),
+            vm((512, 128), F32), vm((2, 8, 32, 128), F32), vm((2, 32, 8, 128), F32), vm((4, 256, 128), F32),
             vm((2, 256, 256), BF16), vm((16, 32, 128), F32), vm((16, 32, 128), F32), vm((2, 128, 512), BF16),
             vm((2, 32, 512), F32),
             vm((2, 32, 512), F32), vm((2, 32, 512), F32), vm((2, 32, 512), F32), vm((2, 32, 512), F32),

time: 69 us -> 69 us (level)
  no operation moved by 1% of the time
where the time goes in v4:
time: 69 us; the launch traced here: 68.8 us
  Pallas kernels  68.2 us (99%)
    pallas_call x1, Pallas kernels, per_device(): pl.pallas_call(kernel, out_shape=jax.ShapeDtypeStruct((4, 32, 512), F32),...  66.4 us
    pallas_call x1, Pallas kernels, per_device(): pl.pallas_call(finish, out_shape=(wide, wide, wide) + (jax.ShapeDtypeStru...  1.79 us

profile of v4, /device:TPU:1, one launch (start us, length us, event | category | flops | bytes accessed | tf_op | source)
XLA Modules:
  0.0 68.8 jit_solution(1037675076144672840)
XLA Ops:
  0.6 66.4 %spectral_backward.1.outs = f32[4,32,512]{2,1,0:T(8,128)} custom-call(f32[32,512]{1,0:T(8,128)} %x_re.3, f32[32,512]{1,0:T(8,128)} %x_im.3, f32[32,512]{1,0:T(8,128)} %gate.3, f32[32,512]{1,0:T(8,128)} %cot_re.1, f32[32,512]{1,0:T(8,128)} %cot_im.1, f32[2,16,512]{2,1,0:T(8,128)} %filt_re.1, f32[2,16,512]{2,1,0:T(8,128)} %filt_im.1, ...), custom_call_target="tpu_custom_call" | custom-call | tf_op jit(solution)/shard_map/spectral_backward/pallas_call | solution.py:389
  67.0 1.8 %products.1 = (f32[32,512]{1,0:T(8,128)}, f32[32,512]{1,0:T(8,128)}, f32[32,512]{1,0:T(8,128)}, f32[2,16,512]{2,1,0:T(8,128)}, f32[2,16,512]{2,1,0:T(8,128)}) custom-call(f32[32,512]{1,0:T(8,128)} %x_re.3, f32[32,512]{1,0:T(8,128)} %x_im.3, f32[32,512]{1,0:T(8,128)} %gate.3, f32[4,32,512]{2,1,0:T(8,128)} %spectral_backward.1.outs), custom_call_target="tpu_custom_call" | custom-call | tf_op jit(solution)/shard_map/products/pallas_call | solution.py:415
